TPU v7x, 32 devices: a whole 2x2x4 slice. The times are simulated.
32 devices in a mesh: xg: 4 (over z), yd: 8 (over y, x, core).
Axes of the slice: x: 2, y: 2, z: 4, core: 2. Of those that a mesh axis runs over, the one named last changes fastest.
Arguments:
- cotangent: float32 [2, 1, 2048, 1024], P(None, None, 'xg', 'yd'), may hold values from -240 to 240
- x_diffusivity: float32 [2, 1, 2048, 1024], P(None, None, 'xg', 'yd'), may hold values from 0.05 to 2
- x_speed: float32 [1, 2048, 1024], P(None, 'xg', 'yd'), may hold values from 1024 to 8192
- x_upwind: int32 [1, 2048, 1024], P(None, 'xg', 'yd'), may hold values from 0 to 1
- y_diffusivity: float32 [2, 1, 2048, 1024], P(None, None, 'xg', 'yd'), may hold values from 64 to 2048
- y_speed: float32 [1, 2048, 1024], P(None, 'xg', 'yd'), may hold values from 1024 to 8192
- y_upwind: int32 [1, 2048, 1024], P(None, 'xg', 'yd'), may hold values from 0 to 1
- coupling: float32 [4, 1, 2048, 1024], P(None, None, 'xg', 'yd'), may hold values from -1.8 to 2, as said below
- x_codes: int32 [1, 1024], P(None, 'yd'), may hold values from 0 to 2
- y_codes: int32 [1, 2048], P(None, 'xg'), may hold values from 0 to 2
Outputs:
- state_grad: float32 [2, 1, 2048, 1024], P(None, None, 'xg', 'yd')
Inputs may be any that keep to these rules, and one draw needn't show every extreme that they name: `coupling`: coupling_0 and coupling_3 lie in 0.01 to 2; |coupling_2| is at most 0.9 coupling_0 and |coupling_1| at most 0.9 coupling_3.
All inputs are finite; a program needn't handle non-finite values.
Results may differ from a plain program's by a relative error of at most 0.0003.
Values sent between devices are 32-bit elements; how exact they have to be, the bound alone decides.
A program may use at most 128 MiB of HBM per device.

v0:
```python
import functools

import jax
import jax.numpy as jnp
from jax import lax
from jax.experimental import pallas as pl
from jax.experimental.pallas import tpu as pltpu
from jax.sharding import PartitionSpec as P

LANES = 128
SUB = 8
F32 = jnp.float32


def mat_mul(p, q):
    return (
        p[0] * q[0] + p[1] * q[2],
        p[0] * q[1] + p[1] * q[3],
        p[2] * q[0] + p[3] * q[2],
        p[2] * q[1] + p[3] * q[3],
    )


def mat_vec(p, v):
    return (p[0] * v[0] + p[1] * v[1], p[2] * v[0] + p[3] * v[1])


def mat_inv(p):
    inv = 1.0 / (p[0] * p[3] - p[1] * p[2])
    return (p[3] * inv, -p[1] * inv, -p[2] * inv, p[0] * inv)


def add(p, q):
    return tuple(x + y for x, y in zip(p, q))


def chunked(lo, hi, unroll, body, carry):
    whole = (hi - lo) // unroll

    def group(step, c):
        for u in range(unroll):
            c = body(lo + step * unroll + u, c)
        return c

    carry = lax.fori_loop(0, whole, group, carry)
    for i in range(lo + whole * unroll, hi):
        carry = body(i, carry)
    return carry


def y_forward(cot, diff, speed, upwind, codes, f_out, g_out, h_out, pack, low, left, right, rhs, first):
    rows_x, length = cot.shape[2], cot.shape[3]
    chunks = rows_x // LANES
    width = 2 * chunks
    boundary = lax.axis_index("yd") == 0
    for j in range(chunks):
        span = pl.ds(j * LANES, LANES)
        sp = speed[0, span, :]
        sm = sp * upwind[0, span, :].astype(F32)
        smt = sm.T
        snt = (sp - sm).T
        for c in range(2):
            slot = c * chunks + j
            df = diff[c, 0, span, :].T
            where = pl.ds(slot, length, stride=width)
            left[where, :] = smt + df
            right[where, :] = snt + df
            rhs[where, :] = cot[c, 0, span, :].T
            first[0, pl.ds(slot, 1), :] = snt[0:1, :]
            first[1, pl.ds(slot, 1), :] = df[0:1, :]
            first[2, pl.ds(slot, 1), :] = codes[0:1, span].astype(F32)

    def at(ref, i):
        return ref[pl.ds(pl.multiple_of(i * width, width), width), :]

    kind = first[2]
    edge = jnp.where(kind >= 0.5, first[0], 0.0) + jnp.where(jnp.abs(kind - 1.0) < 0.5, first[1], 0.0)
    r0 = jnp.where(boundary, edge, at(right, 0))
    right[pl.ds(0, width), :] = r0

    def step(i, carry):
        g, m, h, a_all, k_all, v_all = carry
        a = at(left, i + 1)
        r = at(right, i)
        rm = 1.0 + r * m
        rg = r * g
        inv = 1.0 / ((rm + a) + rg)
        m = rm * inv
        g = rg * inv
        h = (at(rhs, i) + r * h) * inv
        f = a * inv
        f_out[i] = f
        g_out[i] = g
        h_out[i] = h
        return (g, m, h, a_all * f, k_all + a_all * m, v_all + a_all * h)

    zero = jnp.zeros((width, LANES), F32)
    one = zero + 1.0
    g, m, h, a_all, k_all, v_all = chunked(0, length - 1, 8, step, (one, zero, zero, one, zero, zero))
    r = at(right, length - 1)
    a0 = at(left, 0)
    pack[0] = r * g
    pack[1] = 1.0 + r * m
    pack[2] = at(rhs, length - 1) + r * h
    pack[3] = a0 * a_all
    pack[4] = a0 * k_all
    pack[5] = a0 * v_all
    f_out[length - 1] = zero
    g_out[length - 1] = zero
    h_out[length - 1] = zero


def gather_kernel(axis, count, src, out, send_sem, recv_sem, own_sem):
    me = lax.axis_index(axis)
    barrier = pltpu.get_barrier_semaphore()
    for k in range(1, count):
        pl.semaphore_signal(
            barrier, inc=1, device_id={axis: lax.rem(me + k, count)}, device_id_type=pl.DeviceIdType.MESH
        )
    own = pltpu.make_async_copy(src, out.at[me], own_sem)
    own.start()
    pl.semaphore_wait(barrier, count - 1)
    copies = []
    for k in range(1, count):
        copy = pltpu.make_async_remote_copy(
            src_ref=src,
            dst_ref=out.at[me],
            send_sem=send_sem.at[k - 1],
            recv_sem=recv_sem.at[k - 1],
            device_id={axis: lax.rem(me + k, count)},
            device_id_type=pl.DeviceIdType.MESH,
        )
        copy.start()
        copies.append(copy)
    own.wait()
    for copy in copies:
        copy.wait()


def gather(axis, count, block, ident):
    return pl.pallas_call(
        functools.partial(gather_kernel, axis, count),
        out_shape=jax.ShapeDtypeStruct((count,) + block.shape, block.dtype),
        in_specs=[pl.BlockSpec(memory_space=pltpu.VMEM)],
        out_specs=pl.BlockSpec(memory_space=pltpu.VMEM),
        scratch_shapes=[
            pltpu.SemaphoreType.DMA((max(count - 1, 1),)),
            pltpu.SemaphoreType.DMA((max(count - 1, 1),)),
            pltpu.SemaphoreType.DMA,
        ],
        compiler_params=pltpu.CompilerParams(collective_id=ident, has_side_effects=True),
        name="gather_" + axis,
    )(block)


def middle(ny, packs, fy, gy, hy, diff, speed, upwind, coupling, codes,
           fx, gx, hx, chain, pack, q_all, lines, weights, edges):
    width = fy.shape[1]
    length = fy.shape[0]
    zero = jnp.zeros((width, LANES), F32)
    slack, h = zero + 1.0, zero
    factors = []
    for j in range(ny):
        lo, sg, v = packs[j, 0], packs[j, 1], packs[j, 2]
        up = zero
        if j + 1 < ny:
            up = packs[j + 1, 3]
            sg = sg + packs[j + 1, 4]
            v = v + packs[j + 1, 5]
        t = sg + lo * slack
        inv = 1.0 / (t + up)
        slack = t * inv
        h = (v + lo * h) * inv
        factors.append((up * inv, h))
    q = zero
    for j in reversed(range(ny)):
        f, h = factors[j]
        q = f * q + h
        q_all[j + 1] = q
    q_all[0] = zero
    me = lax.axis_index("yd")
    p = q_all[me]
    q = q_all[me + 1]

    def put(i, value):
        lines[pl.ds(pl.multiple_of(i * width, width), width), :] = value

    put(length - 1, q)

    def back(n, w):
        i = length - 2 - n
        w = fy[i] * w + (gy[i] * p + hy[i])
        put(i, w)
        return w

    chunked(0, length - 1, 8, back, q)
    rows_x = diff.shape[2]
    chunks = rows_x // LANES
    for c in range(2):
        for j in range(chunks):
            block = lines[pl.ds(c * chunks + j, length, stride=width), :]
            weights[c, pl.ds(j * LANES, LANES), :] = block.T

    depth = rows_x // SUB
    at_start = lax.axis_index("xg") == 0

    def rows(k):
        return pl.ds(k, SUB, stride=depth)

    def lefts(k):
        sm = speed[0, rows(k), :] * upwind[0, rows(k), :].astype(F32)
        return (sm + diff[0, 0, rows(k), :], sm + diff[1, 0, rows(k), :])

    def rights(k):
        sp = speed[0, rows(k), :]
        sn = sp - sp * upwind[0, rows(k), :].astype(F32)
        return (sn, diff[0, 0, rows(k), :], diff[1, 0, rows(k), :])

    def sigma(k):
        return (
            1.0 + 0.5 * coupling[0, 0, rows(k), :],
            0.5 * coupling[2, 0, rows(k), :],
            0.5 * coupling[1, 0, rows(k), :],
            1.0 + 0.5 * coupling[3, 0, rows(k), :],
        )

    def step(k, carry, r):
        g, m, h, a_all, k_all, v_all = carry
        a = lefts(k + 1)
        sg = sigma(k)
        rm = (sg[0] + r[0] * m[0], sg[1] + r[0] * m[1], sg[2] + r[1] * m[2], sg[3] + r[1] * m[3])
        rg = (r[0] * g[0], r[0] * g[1], r[1] * g[2], r[1] * g[3])
        d = (rm[0] + a[0] + rg[0], rm[1] + rg[1], rm[2] + rg[2], rm[3] + a[1] + rg[3])
        inv = mat_inv(d)
        m = mat_mul(inv, rm)
        g = mat_mul(inv, rg)
        f = (inv[0] * a[0], inv[1] * a[1], inv[2] * a[0], inv[3] * a[1])
        h = mat_vec(inv, tuple(weights[c, rows(k), :] + r[c] * h[c] for c in range(2)))
        for e in range(4):
            fx[k, e] = f[e]
            gx[k, e] = g[e]
        for c in range(2):
            hx[k, c] = h[c]
        return (
            g, m, h, mat_mul(a_all, f), add(k_all, mat_mul(a_all, m)), add(v_all, mat_vec(a_all, h)),
        )

    zero = jnp.zeros((SUB, LANES), F32)
    one = zero + 1.0
    unit = (one, zero, zero, one)
    none = (zero,) * 4
    kind = codes[0:1, :]
    top = (lax.broadcasted_iota(jnp.int32, (SUB, LANES), 0) == 0) & at_start
    sn, d0, d1 = rights(0)
    vented = (kind >= 1).astype(F32)
    opened = (kind == 1).astype(F32)
    r_first = tuple(jnp.where(top, vented * sn + opened * d, sn + d) for d in (d0, d1))
    carry = step(0, (unit, none, (zero, zero), unit, none, (zero, zero)), r_first)

    def inner(k, c):
        sn, d0, d1 = rights(k)
        return step(k, c, (sn + d0, sn + d1))

    g, m, h, a_all, k_all, v_all = chunked(1, depth - 1, 2, inner, carry)
    sn, d0, d1 = rights(depth - 1)
    r = (sn + d0, sn + d1)
    sg = sigma(depth - 1)
    rr = (r[0], r[0], r[1], r[1])
    a0 = lefts(0)
    aa = (a0[0], a0[0], a0[1], a0[1])
    for e in range(4):
        edges[e] = rr[e] * g[e]
        edges[4 + e] = sg[e] + rr[e] * m[e]
        edges[10 + e] = aa[e] * a_all[e]
        edges[14 + e] = aa[e] * k_all[e]
    for c in range(2):
        edges[8 + c] = weights[c, rows(depth - 1), :] + r[c] * h[c]
        edges[18 + c] = a0[c] * v_all[c]

    def edge(first, n, s):
        return tuple(edges[first + e, pl.ds(s, 1), :] for e in range(n))

    zrow = jnp.zeros((1, LANES), F32)
    orow = zrow + 1.0
    g, m, h = (orow, zrow, zrow, orow), (zrow,) * 4, (zrow, zrow)
    a_all, k_all, v_all = edge(10, 4, 0), edge(14, 4, 0), edge(18, 2, 0)
    for s in range(SUB - 1):
        lo, up = edge(0, 4, s), edge(10, 4, s + 1)
        sg = add(edge(4, 4, s), edge(14, 4, s + 1))
        v = add(edge(8, 2, s), edge(18, 2, s + 1))
        rm = add(sg, mat_mul(lo, m))
        rg = mat_mul(lo, g)
        inv = mat_inv(add(add(rm, up), rg))
        m, g, f = mat_mul(inv, rm), mat_mul(inv, rg), mat_mul(inv, up)
        h = mat_vec(inv, add(v, mat_vec(lo, h)))
        for e in range(4):
            chain[s, pl.ds(e, 1), :] = f[e]
            chain[s, pl.ds(4 + e, 1), :] = g[e]
        for c in range(2):
            chain[s, pl.ds(8 + c, 1), :] = h[c]
        k_all = add(k_all, mat_mul(a_all, m))
        v_all = add(v_all, mat_vec(a_all, h))
        a_all = mat_mul(a_all, f)
    last = SUB - 1
    lo = edge(0, 4, last)
    sent = (
        mat_mul(lo, g)
        + add(edge(4, 4, last), mat_mul(lo, m))
        + add(edge(8, 2, last), mat_vec(lo, h))
        + a_all
        + k_all
        + v_all
    )
    for e, row in enumerate(sent):
        pack[pl.ds(e, 1), :] = row
    for e in range(len(sent), pack.shape[0]):
        pack[pl.ds(e, 1), :] = zrow


def x_backward(nx, packs, chain, fx, gx, hx, out, q_all, before, own):
    def row(j, first, n):
        return tuple(packs[j, pl.ds(first + e, 1), :] for e in range(n))

    zrow = jnp.zeros((1, LANES), F32)
    orow = zrow + 1.0
    slack, h = (orow, zrow, zrow, orow), (zrow, zrow)
    factors = []
    for j in range(nx):
        lo, sg, v = row(j, 0, 4), row(j, 4, 4), row(j, 8, 2)
        up = (zrow,) * 4
        if j + 1 < nx:
            up = row(j + 1, 10, 4)
            sg = add(sg, row(j + 1, 14, 4))
            v = add(v, row(j + 1, 18, 2))
        t = add(sg, mat_mul(lo, slack))
        inv = mat_inv(add(t, up))
        slack = mat_mul(inv, t)
        h = mat_vec(inv, add(v, mat_vec(lo, h)))
        factors.append((mat_mul(inv, up), h))
    q = (zrow, zrow)
    for c in range(2):
        q_all[0, pl.ds(c, 1), :] = zrow
    for j in reversed(range(nx)):
        f, h = factors[j]
        q = add(mat_vec(f, q), h)
        for c in range(2):
            q_all[j + 1, pl.ds(c, 1), :] = q[c]
    me = lax.axis_index("xg")
    p = tuple(q_all[me, pl.ds(c, 1), :] for c in range(2))
    q = tuple(q_all[me + 1, pl.ds(c, 1), :] for c in range(2))
    for c in range(2):
        own[c, pl.ds(SUB - 1, 1), :] = q[c]
        before[c, pl.ds(0, 1), :] = p[c]
    for s in reversed(range(SUB - 1)):
        f = tuple(chain[s, pl.ds(e, 1), :] for e in range(4))
        g = tuple(chain[s, pl.ds(4 + e, 1), :] for e in range(4))
        h = tuple(chain[s, pl.ds(8 + c, 1), :] for c in range(2))
        q = add(mat_vec(f, q), add(mat_vec(g, p), h))
        for c in range(2):
            own[c, pl.ds(s, 1), :] = q[c]
            before[c, pl.ds(s + 1, 1), :] = q[c]
    depth = out.shape[2] // SUB
    prev = (before[0], before[1])
    x = (own[0], own[1])

    def put(k, x):
        for c in range(2):
            out[c, 0, pl.ds(k, SUB, stride=depth), :] = x[c]

    put(depth - 1, x)

    def back(n, x):
        k = depth - 2 - n
        f = tuple(fx[k, e] for e in range(4))
        g = tuple(gx[k, e] for e in range(4))
        base = add(mat_vec(g, prev), (hx[k, 0], hx[k, 1]))
        x = add(mat_vec(f, x), base)
        put(k, x)
        return x

    chunked(0, depth - 1, 8, back, x)


def call(body, outs, scratch, args, name):
    whole = pl.BlockSpec(memory_space=pltpu.VMEM)
    return pl.pallas_call(
        body,
        out_shape=[jax.ShapeDtypeStruct(s, F32) for s in outs],
        in_specs=[whole] * len(args),
        out_specs=[whole] * len(outs),
        scratch_shapes=[pltpu.VMEM(s, F32) for s in scratch],
        compiler_params=pltpu.CompilerParams(vmem_limit_bytes=40 * 1024 * 1024),
        name=name,
    )(*args)


def per_device(ny, nx, cotangent, x_diffusivity, x_speed, x_upwind, y_diffusivity, y_speed, y_upwind,
               coupling, x_codes, y_codes):
    rows_x, length = cotangent.shape[2], cotangent.shape[3]
    width = 2 * rows_x // LANES
    depth = rows_x // SUB
    tall = (length * width, LANES)
    fy, gy, hy, pack = call(
        y_forward,
        [(length, width, LANES)] * 3 + [(6, width, LANES)],
        [(8, LANES), tall, tall, tall, (3, width, LANES)],
        [cotangent, y_diffusivity, y_speed, y_upwind, y_codes],
        "y_forward",
    )
    packs = gather("yd", ny, pack, 1)
    fx, gx, hx, chain, pack = call(
        functools.partial(middle, ny),
        [(depth, 4, SUB, LANES), (depth, 4, SUB, LANES), (depth, 2, SUB, LANES),
         (SUB, 16, LANES), (24, LANES)],
        [(ny + 1, width, LANES), tall, (2, rows_x, LANES), (20, SUB, LANES)],
        [packs, fy, gy, hy, x_diffusivity, x_speed, x_upwind, coupling, x_codes],
        "middle",
    )
    packs = gather("xg", nx, pack, 2)
    (out,) = call(
        functools.partial(x_backward, nx),
        [cotangent.shape],
        [(nx + 1, SUB, LANES), (2, SUB, LANES), (2, SUB, LANES)],
        [packs, chain, fx, gx, hx],
        "x_backward",
    )
    return out


def solution(mesh):
    body = functools.partial(per_device, mesh.shape["yd"], mesh.shape["xg"])
    return jax.shard_map(
        body,
        mesh=mesh,
        in_specs=(
            P(None, None, "xg", "yd"),
            P(None, None, "xg", "yd"),
            P(None, "xg", "yd"),
            P(None, "xg", "yd"),
            P(None, None, "xg", "yd"),
            P(None, "xg", "yd"),
            P(None, "xg", "yd"),
            P(None, None, "xg", "yd"),
            P(None, "yd"),
            P(None, "xg"),
        ),
        out_specs=P(None, None, "xg", "yd"),
        check_vma=False,
    )
```

profile of v0, /device:TPU:0, one launch (start us, length us, event | category | flops | bytes accessed | tf_op | source)
XLA Modules:
  0.0 40.6 jit_solution(5901656696238636667)
XLA Ops:
  0.0 1.1 %copy-done.4 = f32[2,1,512,128]{3,2,1,0:T(8,128)S(1)} copy-done((f32[2,1,512,128]{3,2,1,0:T(8,128)S(1)}, f32[2,1,512,128]{3,2,1,0:T(8,128)}, u32[]{:S(2)}) %copy-start.4) | copy-done | bytes 524312
  1.1 1.0 %copy-done.5 = f32[2,1,512,128]{3,2,1,0:T(8,128)S(1)} copy-done((f32[2,1,512,128]{3,2,1,0:T(8,128)S(1)}, f32[2,1,512,128]{3,2,1,0:T(8,128)}, u32[]{:S(2)}) %copy-start.5) | copy-done | bytes 524312
  2.2 0.9 %copy-done.15 = f32[1,512,128]{2,1,0:T(8,128)S(1)} copy-done((f32[1,512,128]{2,1,0:T(8,128)S(1)}, f32[1,512,128]{2,1,0:T(8,128)}, u32[]{:S(2)}) %copy-start.15) | copy-done | bytes 262168
  3.1 0.9 %copy-done.16 = s32[1,512,128]{2,1,0:T(8,128)S(1)} copy-done((s32[1,512,128]{2,1,0:T(8,128)S(1)}, s32[1,512,128]{2,1,0:T(8,128)}, u32[]{:S(2)}) %copy-start.16) | copy-done | bytes 262168
  4.1 0.7 %copy-done.20 = s32[1,512]{1,0:T(1,128)S(1)} copy-done((s32[1,512]{1,0:T(1,128)S(1)}, s32[1,512]{1,0:T(1,128)}, u32[]{:S(2)}) %copy-start.20) | copy-done | bytes 2072
  4.8 2.1 %y_forward.1 = (f32[128,8,128]{2,1,0:T(8,128)S(1)}, f32[128,8,128]{2,1,0:T(8,128)S(1)}, f32[128,8,128]{2,1,0:T(8,128)S(1)}, f32[6,8,128]{2,1,0:T(8,128)S(1)}) custom-call(f32[2,1,512,128]{3,2,1,0:T(8,128)S(1)} %copy-done.4, f32[2,1,512,128]{3,2,1,0:T(8,128)S(1)} %copy-done.5, f32[1,512,128]{2,1,0:T(8,128)S(1)} %copy-done.15, s32[1,512,128]{2,1,0:T(8,128)S(1)} %copy-done.16, ...), custom_call_target="tpu_custom_call" | custom-call | tf_op jit(solution)/shard_map/y_forward/pallas_call | solution.py:386
  6.9 0.8 %copy-done.7 = f32[128,8,128]{2,1,0:T(8,128)} copy-done((f32[128,8,128]{2,1,0:T(8,128)}, f32[128,8,128]{2,1,0:T(8,128)S(1)}, u32[]{:S(2)}) %copy-start.7) | copy-done | bytes 524312
  7.7 0.8 %copy-done.9 = f32[128,8,128]{2,1,0:T(8,128)} copy-done((f32[128,8,128]{2,1,0:T(8,128)}, f32[128,8,128]{2,1,0:T(8,128)S(1)}, u32[]{:S(2)}) %copy-start.9) | copy-done | bytes 524312
  8.5 0.8 %copy-done.11 = f32[128,8,128]{2,1,0:T(8,128)} copy-done((f32[128,8,128]{2,1,0:T(8,128)}, f32[128,8,128]{2,1,0:T(8,128)S(1)}, u32[]{:S(2)}) %copy-start.11) | copy-done | bytes 524312
  9.3 0.6 %copy-done.18 = f32[6,8,128]{2,1,0:T(8,128)} copy-done((f32[6,8,128]{2,1,0:T(8,128)}, f32[6,8,128]{2,1,0:T(8,128)S(1)}, u32[]{:S(2)}) %copy-start.18) | copy-done | bytes 24600
  9.9 8.9 %gather_yd.1.packs = f32[8,6,8,128]{3,2,1,0:T(8,128)} custom-call(f32[6,8,128]{2,1,0:T(8,128)} %copy-done.18), custom_call_target="tpu_custom_call" | custom-call | tf_op jit(solution)/shard_map/gather_yd/pallas_call | solution.py:141
  18.8 0.9 %copy-done.1 = f32[8,6,8,128]{3,2,1,0:T(8,128)S(1)} copy-done((f32[8,6,8,128]{3,2,1,0:T(8,128)S(1)}, f32[8,6,8,128]{3,2,1,0:T(8,128)}, u32[]{:S(2)}) %copy-start.1) | copy-done | bytes 196632
  19.7 1.0 %copy-done.6 = f32[2,1,512,128]{3,2,1,0:T(8,128)S(1)} copy-done((f32[2,1,512,128]{3,2,1,0:T(8,128)S(1)}, f32[2,1,512,128]{3,2,1,0:T(8,128)}, u32[]{:S(2)}) %copy-start.6) | copy-done | bytes 524312
  20.8 1.0 %copy-done.8 = f32[128,8,128]{2,1,0:T(8,128)S(1)} copy-done((f32[128,8,128]{2,1,0:T(8,128)S(1)}, f32[128,8,128]{2,1,0:T(8,128)}, u32[]{:S(2)}) %copy-start.8) | copy-done | bytes 524312
  21.8 1.0 %copy-done.10 = f32[128,8,128]{2,1,0:T(8,128)S(1)} copy-done((f32[128,8,128]{2,1,0:T(8,128)S(1)}, f32[128,8,128]{2,1,0:T(8,128)}, u32[]{:S(2)}) %copy-start.10) | copy-done | bytes 524312
  22.8 1.0 %copy-done.12 = f32[128,8,128]{2,1,0:T(8,128)S(1)} copy-done((f32[128,8,128]{2,1,0:T(8,128)S(1)}, f32[128,8,128]{2,1,0:T(8,128)}, u32[]{:S(2)}) %copy-start.12) | copy-done | bytes 524312
  23.9 0.9 %copy-done.14 = s32[1,512,128]{2,1,0:T(8,128)S(1)} copy-done((s32[1,512,128]{2,1,0:T(8,128)S(1)}, s32[1,512,128]{2,1,0:T(8,128)}, u32[]{:S(2)}) %copy-start.14) | copy-done | bytes 262168
  24.8 3.7 %middle.1 = (f32[64,4,8,128]{3,2,1,0:T(8,128)S(1)}, f32[64,4,8,128]{3,2,1,0:T(8,128)S(1)}, f32[64,2,8,128]{3,2,1,0:T(8,128)S(1)}, f32[8,16,128]{2,1,0:T(8,128)S(1)}, f32[24,128]{1,0:T(8,128)S(1)}) custom-call(f32[8,6,8,128]{3,2,1,0:T(8,128)S(1)} %copy-done.1, f32[128,8,128]{2,1,0:T(8,128)S(1)} %copy-done.8, f32[128,8,128]{2,1,0:T(8,128)S(1)} %copy-done.10, ...), custom_call_target="tpu_custom_call" | custom-call | tf_op jit(solution)/shard_map/middle/pallas_call | solution.py:386
  28.6 0.8 %copy-done.2 = f32[64,2,8,128]{3,2,1,0:T(8,128)} copy-done((f32[64,2,8,128]{3,2,1,0:T(8,128)}, f32[64,2,8,128]{3,2,1,0:T(8,128)S(1)}, u32[]{:S(2)}) %copy-start.2) | copy-done | bytes 524312
  29.4 0.6 %copy-done.19 = f32[24,128]{1,0:T(8,128)} copy-done((f32[24,128]{1,0:T(8,128)}, f32[24,128]{1,0:T(8,128)S(1)}, u32[]{:S(2)}) %copy-start.19) | copy-done | bytes 12312
  30.0 7.4 %gather_xg.1.packs = f32[4,24,128]{2,1,0:T(8,128)} custom-call(f32[24,128]{1,0:T(8,128)} %copy-done.19), custom_call_target="tpu_custom_call" | custom-call | tf_op jit(solution)/shard_map/gather_xg/pallas_call | solution.py:141
  37.4 1.0 %copy-done.3 = f32[64,2,8,128]{3,2,1,0:T(8,128)S(1)} copy-done((f32[64,2,8,128]{3,2,1,0:T(8,128)S(1)}, f32[64,2,8,128]{3,2,1,0:T(8,128)}, u32[]{:S(2)}) %copy-start.3) | copy-done | bytes 524312
  38.4 0.8 %copy-done.17 = f32[4,24,128]{2,1,0:T(8,128)S(1)} copy-done((f32[4,24,128]{2,1,0:T(8,128)S(1)}, f32[4,24,128]{2,1,0:T(8,128)}, u32[]{:S(2)}) %copy-start.17) | copy-done | bytes 49176
  39.2 1.4 %x_backward.1 = f32[2,1,512,128]{3,2,1,0:T(8,128)} custom-call(f32[4,24,128]{2,1,0:T(8,128)S(1)} %copy-done.17, f32[8,16,128]{2,1,0:T(8,128)S(1)} %get-tuple-element.19.chain, f32[64,4,8,128]{3,2,1,0:T(8,128)S(1)} %get-tuple-element.20.fx, f32[64,4,8,128]{3,2,1,0:T(8,128)S(1)} %get-tuple-element.21.gx, f32[64,2,8,128]{3,2,1,0:T(8,128)S(1)} %copy-done.3), custom_call_target="tpu_custom_call" | custom-call | tf_op jit(solution)/shard_map/x_backward/pallas_call | solution.py:386
  (25 shorter events, 0.0 us)
Async XLA Ops:
  0.0 18.8 %copy-start = (f32[4,1,512,128]{3,2,1,0:T(8,128)S(1)}, f32[4,1,512,128]{3,2,1,0:T(8,128)}, u32[]{:S(2)}) copy-start(f32[4,1,512,128]{3,2,1,0:T(8,128)} %coupling.1) | copy-start | bytes 3145732
  0.0 1.1 %copy-start.4 = (f32[2,1,512,128]{3,2,1,0:T(8,128)S(1)}, f32[2,1,512,128]{3,2,1,0:T(8,128)}, u32[]{:S(2)}) copy-start(f32[2,1,512,128]{3,2,1,0:T(8,128)} %cot.1) | copy-start | bytes 1572868
  1.1 1.0 %copy-start.5 = (f32[2,1,512,128]{3,2,1,0:T(8,128)S(1)}, f32[2,1,512,128]{3,2,1,0:T(8,128)}, u32[]{:S(2)}) copy-start(f32[2,1,512,128]{3,2,1,0:T(8,128)} %diff.2) | copy-start | bytes 1572868
  2.2 0.9 %copy-start.15 = (f32[1,512,128]{2,1,0:T(8,128)S(1)}, f32[1,512,128]{2,1,0:T(8,128)}, u32[]{:S(2)}) copy-start(f32[1,512,128]{2,1,0:T(8,128)} %speed.2) | copy-start | bytes 786436
  3.1 0.9 %copy-start.16 = (s32[1,512,128]{2,1,0:T(8,128)S(1)}, s32[1,512,128]{2,1,0:T(8,128)}, u32[]{:S(2)}) copy-start(s32[1,512,128]{2,1,0:T(8,128)} %upwind.2) | copy-start | bytes 786436
  4.1 0.7 %copy-start.20 = (s32[1,512]{1,0:T(1,128)S(1)}, s32[1,512]{1,0:T(1,128)}, u32[]{:S(2)}) copy-start(s32[1,512]{1,0:T(1,128)} %codes.2) | copy-start | bytes 6148
  4.8 14.0 %copy-start.13 = (f32[1,512,128]{2,1,0:T(8,128)S(1)}, f32[1,512,128]{2,1,0:T(8,128)}, u32[]{:S(2)}) copy-start(f32[1,512,128]{2,1,0:T(8,128)} %speed.3) | copy-start | bytes 786436
  6.9 0.8 %copy-start.7 = (f32[128,8,128]{2,1,0:T(8,128)}, f32[128,8,128]{2,1,0:T(8,128)S(1)}, u32[]{:S(2)}) copy-start(f32[128,8,128]{2,1,0:T(8,128)S(1)} %get-tuple-element.15.fy) | copy-start | bytes 1572868
  7.7 0.8 %copy-start.9 = (f32[128,8,128]{2,1,0:T(8,128)}, f32[128,8,128]{2,1,0:T(8,128)S(1)}, u32[]{:S(2)}) copy-start(f32[128,8,128]{2,1,0:T(8,128)S(1)} %get-tuple-element.16.gy) | copy-start | bytes 1572868
  8.5 0.8 %copy-start.11 = (f32[128,8,128]{2,1,0:T(8,128)}, f32[128,8,128]{2,1,0:T(8,128)S(1)}, u32[]{:S(2)}) copy-start(f32[128,8,128]{2,1,0:T(8,128)S(1)} %get-tuple-element.17.hy) | copy-start | bytes 1572868
  9.3 0.6 %copy-start.18 = (f32[6,8,128]{2,1,0:T(8,128)}, f32[6,8,128]{2,1,0:T(8,128)S(1)}, u32[]{:S(2)}) copy-start(f32[6,8,128]{2,1,0:T(8,128)S(1)} %get-tuple-element.14.src) | copy-start | bytes 73732
  9.9 8.9 %copy-start.21 = (s32[1,128]{1,0:T(1,128)S(1)}, s32[1,128]{1,0:T(1,128)}, u32[]{:S(2)}) copy-start(s32[1,128]{1,0:T(1,128)} %codes.3) | copy-start | bytes 1540
  18.8 0.9 %copy-start.1 = (f32[8,6,8,128]{3,2,1,0:T(8,128)S(1)}, f32[8,6,8,128]{3,2,1,0:T(8,128)}, u32[]{:S(2)}) copy-start(f32[8,6,8,128]{3,2,1,0:T(8,128)} %gather_yd.1.packs) | copy-start | bytes 589828
  19.7 1.0 %copy-start.6 = (f32[2,1,512,128]{3,2,1,0:T(8,128)S(1)}, f32[2,1,512,128]{3,2,1,0:T(8,128)}, u32[]{:S(2)}) copy-start(f32[2,1,512,128]{3,2,1,0:T(8,128)} %diff.3) | copy-start | bytes 1572868
  20.8 1.0 %copy-start.8 = (f32[128,8,128]{2,1,0:T(8,128)S(1)}, f32[128,8,128]{2,1,0:T(8,128)}, u32[]{:S(2)}) copy-start(f32[128,8,128]{2,1,0:T(8,128)} %copy-done.7) | copy-start | bytes 1572868
  21.8 1.0 %copy-start.10 = (f32[128,8,128]{2,1,0:T(8,128)S(1)}, f32[128,8,128]{2,1,0:T(8,128)}, u32[]{:S(2)}) copy-start(f32[128,8,128]{2,1,0:T(8,128)} %copy-done.9) | copy-start | bytes 1572868
  22.8 1.0 %copy-start.12 = (f32[128,8,128]{2,1,0:T(8,128)S(1)}, f32[128,8,128]{2,1,0:T(8,128)}, u32[]{:S(2)}) copy-start(f32[128,8,128]{2,1,0:T(8,128)} %copy-done.11) | copy-start | bytes 1572868
  23.9 0.9 %copy-start.14 = (s32[1,512,128]{2,1,0:T(8,128)S(1)}, s32[1,512,128]{2,1,0:T(8,128)}, u32[]{:S(2)}) copy-start(s32[1,512,128]{2,1,0:T(8,128)} %upwind.3) | copy-start | bytes 786436
  28.6 0.8 %copy-start.2 = (f32[64,2,8,128]{3,2,1,0:T(8,128)}, f32[64,2,8,128]{3,2,1,0:T(8,128)S(1)}, u32[]{:S(2)}) copy-start(f32[64,2,8,128]{3,2,1,0:T(8,128)S(1)} %get-tuple-element.22.hx) | copy-start | bytes 1572868
  29.4 0.6 %copy-start.19 = (f32[24,128]{1,0:T(8,128)}, f32[24,128]{1,0:T(8,128)S(1)}, u32[]{:S(2)}) copy-start(f32[24,128]{1,0:T(8,128)S(1)} %get-tuple-element.18.src) | copy-start | bytes 36868
  37.4 1.0 %copy-start.3 = (f32[64,2,8,128]{3,2,1,0:T(8,128)S(1)}, f32[64,2,8,128]{3,2,1,0:T(8,128)}, u32[]{:S(2)}) copy-start(f32[64,2,8,128]{3,2,1,0:T(8,128)} %copy-done.2) | copy-start | bytes 1572868
  38.4 0.8 %copy-start.17 = (f32[4,24,128]{2,1,0:T(8,128)S(1)}, f32[4,24,128]{2,1,0:T(8,128)}, u32[]{:S(2)}) copy-start(f32[4,24,128]{2,1,0:T(8,128)} %gather_xg.1.packs) | copy-start | bytes 147460
where the time goes:
time: 41.3 us; the launch traced here: 40.6 us
  Pallas kernels  23.5 us (57%)
  local copies, waits for them, and re-layouts  17 us (41%)
    unnamed x44, local copies, waits for them, and re-layouts  17 us
    pallas_call x2, Pallas kernels, gather(): pl.pallas_call(functools.partial(gather_kernel, axis, count), out_shape=j...  16.2 us
    pallas_call x3, Pallas kernels, call(): pl.pallas_call(body, out_shape=[jax.ShapeDtypeStruct(s, F32) for s in out...  7.24 us

commit v1 on v0

v1 whole, which is shorter than its diff:
```python
import functools

import jax
import jax.numpy as jnp
from jax import lax
from jax.experimental import pallas as pl
from jax.experimental.pallas import tpu as pltpu
from jax.sharding import PartitionSpec as P

LANES = 128
SUB = 8
F32 = jnp.float32


def mat_mul(p, q):
    return (
        p[0] * q[0] + p[1] * q[2],
        p[0] * q[1] + p[1] * q[3],
        p[2] * q[0] + p[3] * q[2],
        p[2] * q[1] + p[3] * q[3],
    )


def mat_vec(p, v):
    return (p[0] * v[0] + p[1] * v[1], p[2] * v[0] + p[3] * v[1])


def mat_inv(p):
    inv = 1.0 / (p[0] * p[3] - p[1] * p[2])
    return (p[3] * inv, -p[1] * inv, -p[2] * inv, p[0] * inv)


def add(p, q):
    return tuple(x + y for x, y in zip(p, q))


def chunked(lo, hi, unroll, body, carry):
    whole = (hi - lo) // unroll

    def group(step, c):
        for u in range(unroll):
            c = body(lo + step * unroll + u, c)
        return c

    carry = lax.fori_loop(0, whole, group, carry)
    for i in range(lo + whole * unroll, hi):
        carry = body(i, carry)
    return carry


def y_forward(cot, diff, speed, upwind, codes, f_out, g_out, h_out, pack, left, right, rhs, first):
    rows_x, length = cot.shape[2], cot.shape[3]
    chunks = rows_x // LANES
    width = 2 * chunks
    boundary = lax.axis_index("yd") == 0
    for j in range(chunks):
        span = pl.ds(j * LANES, LANES)
        sp = speed[0, span, :]
        sm = sp * upwind[0, span, :].astype(F32)
        smt = sm.T
        snt = (sp - sm).T
        for c in range(2):
            slot = c * chunks + j
            df = diff[c, 0, span, :].T
            where = pl.ds(slot, length, stride=width)
            left[where, :] = smt + df
            right[where, :] = snt + df
            rhs[where, :] = cot[c, 0, span, :].T
            first[0, pl.ds(slot, 1), :] = snt[0:1, :]
            first[1, pl.ds(slot, 1), :] = df[0:1, :]
            first[2, pl.ds(slot, 1), :] = codes[0:1, span].astype(F32)

    def at(ref, i):
        return ref[pl.ds(pl.multiple_of(i * width, width), width), :]

    kind = first[2]
    edge = jnp.where(kind >= 0.5, first[0], 0.0) + jnp.where(jnp.abs(kind - 1.0) < 0.5, first[1], 0.0)
    r0 = jnp.where(boundary, edge, at(right, 0))
    right[pl.ds(0, width), :] = r0

    def step(i, carry):
        g, m, h, a_all, k_all, v_all = carry
        a = at(left, i + 1)
        r = at(right, i)
        rm = 1.0 + r * m
        rg = r * g
        inv = 1.0 / ((rm + a) + rg)
        m = rm * inv
        g = rg * inv
        h = (at(rhs, i) + r * h) * inv
        f = a * inv
        f_out[i] = f
        g_out[i] = g
        h_out[i] = h
        return (g, m, h, a_all * f, k_all + a_all * m, v_all + a_all * h)

    zero = jnp.zeros((width, LANES), F32)
    one = zero + 1.0
    g, m, h, a_all, k_all, v_all = chunked(0, length - 1, 8, step, (one, zero, zero, one, zero, zero))
    r = at(right, length - 1)
    a0 = at(left, 0)
    pack[0] = r * g
    pack[1] = 1.0 + r * m
    pack[2] = at(rhs, length - 1) + r * h
    pack[3] = a0 * a_all
    pack[4] = a0 * k_all
    pack[5] = a0 * v_all


def y_interfaces(ny, packs, q_all, width):
    zero = jnp.zeros((width, LANES), F32)
    slack, h = zero + 1.0, zero
    factors = []
    for j in range(ny):
        lo, sg, v = packs[j, 0], packs[j, 1], packs[j, 2]
        up = zero
        if j + 1 < ny:
            up = packs[j + 1, 3]
            sg = sg + packs[j + 1, 4]
            v = v + packs[j + 1, 5]
        t = sg + lo * slack
        inv = 1.0 / (t + up)
        slack = t * inv
        h = (v + lo * h) * inv
        factors.append((up * inv, h))
    q = zero
    for j in reversed(range(ny)):
        f, h = factors[j]
        q = f * q + h
        q_all[j + 1] = q
    q_all[0] = zero
    me = lax.axis_index("yd")
    return q_all[me], q_all[me + 1]


def y_backward(p, q, fy, gy, hy, lines, weights):
    length, width = fy.shape[0], fy.shape[1]

    def put(i, value):
        lines[pl.ds(pl.multiple_of(i * width, width), width), :] = value

    put(length - 1, q)

    def back(n, w):
        i = length - 2 - n
        w = fy[i] * w + (gy[i] * p + hy[i])
        put(i, w)
        return w

    chunked(0, length - 1, 8, back, q)
    chunks = width // 2
    for c in range(2):
        for j in range(chunks):
            block = lines[pl.ds(c * chunks + j, length, stride=width), :]
            weights[c, pl.ds(j * LANES, LANES), :] = block.T


def x_coefficients(diff, speed, upwind, coupling, codes, fx, gx, ix, nx_, ax, edges):
    depth = diff.shape[2] // SUB
    at_start = lax.axis_index("xg") == 0

    def rows(k):
        return pl.ds(k, SUB, stride=depth)

    def lefts(k):
        sm = speed[0, rows(k), :] * upwind[0, rows(k), :].astype(F32)
        return (sm + diff[0, 0, rows(k), :], sm + diff[1, 0, rows(k), :])

    def rights(k):
        sp = speed[0, rows(k), :]
        sn = sp - sp * upwind[0, rows(k), :].astype(F32)
        return (sn, diff[0, 0, rows(k), :], diff[1, 0, rows(k), :])

    def sigma(k):
        return (
            1.0 + 0.5 * coupling[0, 0, rows(k), :],
            0.5 * coupling[2, 0, rows(k), :],
            0.5 * coupling[1, 0, rows(k), :],
            1.0 + 0.5 * coupling[3, 0, rows(k), :],
        )

    def step(k, carry, r):
        g, m, a_all, k_all = carry
        a = lefts(k + 1)
        sg = sigma(k)
        rm = (sg[0] + r[0] * m[0], sg[1] + r[0] * m[1], sg[2] + r[1] * m[2], sg[3] + r[1] * m[3])
        rg = (r[0] * g[0], r[0] * g[1], r[1] * g[2], r[1] * g[3])
        d = (rm[0] + a[0] + rg[0], rm[1] + rg[1], rm[2] + rg[2], rm[3] + a[1] + rg[3])
        inv = mat_inv(d)
        m = mat_mul(inv, rm)
        g = mat_mul(inv, rg)
        f = (inv[0] * a[0], inv[1] * a[1], inv[2] * a[0], inv[3] * a[1])
        n = (inv[0] * r[0], inv[1] * r[1], inv[2] * r[0], inv[3] * r[1])
        for e in range(4):
            fx[k, e] = f[e]
            gx[k, e] = g[e]
            ix[k, e] = inv[e]
            nx_[k, e] = n[e]
            ax[k, e] = a_all[e]
        return (g, m, mat_mul(a_all, f), add(k_all, mat_mul(a_all, m)))

    zero = jnp.zeros((SUB, LANES), F32)
    one = zero + 1.0
    unit = (one, zero, zero, one)
    none = (zero,) * 4
    kind = codes[0:1, :]
    top = (lax.broadcasted_iota(jnp.int32, (SUB, LANES), 0) == 0) & at_start
    sn, d0, d1 = rights(0)
    vented = (kind >= 1).astype(F32)
    opened = (kind == 1).astype(F32)
    r_first = tuple(jnp.where(top, vented * sn + opened * d, sn + d) for d in (d0, d1))
    carry = step(0, (unit, none, unit, none), r_first)

    def inner(k, c):
        sn, d0, d1 = rights(k)
        return step(k, c, (sn + d0, sn + d1))

    g, m, a_all, k_all = chunked(1, depth - 1, 2, inner, carry)
    sn, d0, d1 = rights(depth - 1)
    r = (sn + d0, sn + d1)
    sg = sigma(depth - 1)
    rr = (r[0], r[0], r[1], r[1])
    a0 = lefts(0)
    aa = (a0[0], a0[0], a0[1], a0[1])
    for e in range(4):
        edges[e] = rr[e] * g[e]
        edges[4 + e] = sg[e] + rr[e] * m[e]
        edges[8 + e] = aa[e] * a_all[e]
        edges[12 + e] = aa[e] * k_all[e]
    for c in range(2):
        edges[20 + c] = a0[c]
        edges[22 + c] = r[c]


def edge_rows(edges, first, n, s):
    return tuple(edges[first + e, pl.ds(s, 1), :] for e in range(n))


def x_chain_coefficients(edges, chain, pack, me):
    zrow = jnp.zeros((1, LANES), F32)
    orow = zrow + 1.0
    g, m = (orow, zrow, zrow, orow), (zrow,) * 4
    a_all, k_all = edge_rows(edges, 8, 4, 0), edge_rows(edges, 12, 4, 0)
    for s in range(SUB - 1):
        lo, up = edge_rows(edges, 0, 4, s), edge_rows(edges, 8, 4, s + 1)
        sg = add(edge_rows(edges, 4, 4, s), edge_rows(edges, 12, 4, s + 1))
        rm = add(sg, mat_mul(lo, m))
        rg = mat_mul(lo, g)
        inv = mat_inv(add(add(rm, up), rg))
        m, g, f = mat_mul(inv, rm), mat_mul(inv, rg), mat_mul(inv, up)
        for e in range(4):
            chain[s, pl.ds(e, 1), :] = f[e]
            chain[s, pl.ds(4 + e, 1), :] = g[e]
            chain[s, pl.ds(8 + e, 1), :] = inv[e]
            chain[s, pl.ds(12 + e, 1), :] = a_all[e]
        k_all = add(k_all, mat_mul(a_all, m))
        a_all = mat_mul(a_all, f)
    lo = edge_rows(edges, 0, 4, SUB - 1)
    sent = mat_mul(lo, g) + add(edge_rows(edges, 4, 4, SUB - 1), mat_mul(lo, m)) + a_all + k_all
    for e, row in enumerate(sent):
        pack[me, pl.ds(e, 1), :] = row


def x_values(weights, ix, nx_, ax, hx, edges):
    depth = weights.shape[1] // SUB

    def step(k, carry):
        h, v_all = carry
        w = tuple(weights[c, pl.ds(k, SUB, stride=depth), :] for c in range(2))
        base = mat_vec(tuple(ix[k, e] for e in range(4)), w)
        n = tuple(nx_[k, e] for e in range(4))
        a_all = tuple(ax[k, e] for e in range(4))
        h = ((base[0] + n[0] * h[0]) + n[1] * h[1], (base[1] + n[2] * h[0]) + n[3] * h[1])
        for c in range(2):
            hx[k, c] = h[c]
        return h, add(v_all, mat_vec(a_all, h))

    zero = jnp.zeros((SUB, LANES), F32)
    h, v_all = chunked(0, depth - 1, 7, step, ((zero, zero), (zero, zero)))
    for c in range(2):
        edges[16 + c] = weights[c, pl.ds(depth - 1, SUB, stride=depth), :] + edges[22 + c] * h[c]
        edges[18 + c] = edges[20 + c] * v_all[c]


def x_chain_values(edges, chain, sums, pack, me):
    zrow = jnp.zeros((1, LANES), F32)
    h = (zrow, zrow)
    v_all = edge_rows(edges, 18, 2, 0)
    for s in range(SUB - 1):
        lo = edge_rows(edges, 0, 4, s)
        v = add(edge_rows(edges, 16, 2, s), edge_rows(edges, 18, 2, s + 1))
        inv = tuple(chain[s, pl.ds(8 + e, 1), :] for e in range(4))
        a_all = tuple(chain[s, pl.ds(12 + e, 1), :] for e in range(4))
        h = mat_vec(inv, add(v, mat_vec(lo, h)))
        for c in range(2):
            sums[s, pl.ds(c, 1), :] = h[c]
        v_all = add(v_all, mat_vec(a_all, h))
    lo = edge_rows(edges, 0, 4, SUB - 1)
    sent = add(edge_rows(edges, 16, 2, SUB - 1), mat_vec(lo, h)) + v_all
    for e in range(SUB):
        pack[me, pl.ds(e, 1), :] = sent[e] if e < len(sent) else zrow


def x_backward(nx, coefs, values, chain, sums, fx, gx, hx, out, q_all, before, own):
    def row(ref, j, first, n):
        return tuple(ref[j, pl.ds(first + e, 1), :] for e in range(n))

    zrow = jnp.zeros((1, LANES), F32)
    orow = zrow + 1.0
    slack, h = (orow, zrow, zrow, orow), (zrow, zrow)
    factors = []
    for j in range(nx):
        lo, sg, v = row(coefs, j, 0, 4), row(coefs, j, 4, 4), row(values, j, 0, 2)
        up = (zrow,) * 4
        if j + 1 < nx:
            up = row(coefs, j + 1, 8, 4)
            sg = add(sg, row(coefs, j + 1, 12, 4))
            v = add(v, row(values, j + 1, 2, 2))
        t = add(sg, mat_mul(lo, slack))
        inv = mat_inv(add(t, up))
        slack = mat_mul(inv, t)
        h = mat_vec(inv, add(v, mat_vec(lo, h)))
        factors.append((mat_mul(inv, up), h))
    q = (zrow, zrow)
    for c in range(2):
        q_all[0, pl.ds(c, 1), :] = zrow
    for j in reversed(range(nx)):
        f, h = factors[j]
        q = add(mat_vec(f, q), h)
        for c in range(2):
            q_all[j + 1, pl.ds(c, 1), :] = q[c]
    me = lax.axis_index("xg")
    p = tuple(q_all[me, pl.ds(c, 1), :] for c in range(2))
    q = tuple(q_all[me + 1, pl.ds(c, 1), :] for c in range(2))
    for c in range(2):
        own[c, pl.ds(SUB - 1, 1), :] = q[c]
        before[c, pl.ds(0, 1), :] = p[c]
    for s in reversed(range(SUB - 1)):
        f = tuple(chain[s, pl.ds(e, 1), :] for e in range(4))
        g = tuple(chain[s, pl.ds(4 + e, 1), :] for e in range(4))
        h = tuple(sums[s, pl.ds(c, 1), :] for c in range(2))
        q = add(mat_vec(f, q), add(mat_vec(g, p), h))
        for c in range(2):
            own[c, pl.ds(s, 1), :] = q[c]
            before[c, pl.ds(s + 1, 1), :] = q[c]
    depth = out.shape[1] // SUB
    prev = (before[0], before[1])
    x = (own[0], own[1])

    def put(k, x):
        for c in range(2):
            out[c, pl.ds(k, SUB, stride=depth), :] = x[c]

    put(depth - 1, x)

    def back(n, x):
        k = depth - 2 - n
        f = tuple(fx[k, e] for e in range(4))
        g = tuple(gx[k, e] for e in range(4))
        base = add(mat_vec(g, prev), (hx[k, 0], hx[k, 1]))
        x = add(mat_vec(f, x), base)
        put(k, x)
        return x

    chunked(0, depth - 1, 8, back, x)


def sends(axis, count, ref, send_sem, recv_sem):
    me = lax.axis_index(axis)
    return [
        pltpu.make_async_remote_copy(
            src_ref=ref.at[me],
            dst_ref=ref.at[me],
            send_sem=send_sem.at[k - 1],
            recv_sem=recv_sem.at[k - 1],
            device_id={axis: lax.rem(me + k, count)},
            device_id_type=pl.DeviceIdType.MESH,
        )
        for k in range(1, count)
    ]


def kernel(ny, nx, *refs):
    sources, out_hbm = refs[:10], refs[10]
    held = refs[11:21]
    (fy, gy, hy, left, right, rhs, first, y_packs, q_y, weights, fx, gx, ix, nx_, ax, hx, edges,
     chain, sums, x_coefs, x_vals, q_x, before, own, out,
     in_sem, y_send, y_recv, c_send, c_recv, v_send, v_recv, out_sem) = refs[21:]
    cot, x_diff, x_speed, x_up, y_diff, y_speed, y_up, coupling, x_codes, y_codes = held
    loads = [pltpu.make_async_copy(s, d, in_sem.at[i]) for i, (s, d) in enumerate(zip(sources, held))]
    y_order, x_order = (5, 6, 4, 0, 9), (2, 3, 1, 7, 8)
    for i in y_order + x_order:
        loads[i].start()
    barrier = pltpu.get_barrier_semaphore()
    for axis, count in (("yd", ny), ("xg", nx)):
        for k in range(1, count):
            peer = lax.rem(lax.axis_index(axis) + k, count)
            pl.semaphore_signal(barrier, inc=1, device_id={axis: peer}, device_id_type=pl.DeviceIdType.MESH)
    for i in y_order:
        loads[i].wait()
    me_y, me_x = lax.axis_index("yd"), lax.axis_index("xg")
    y_forward(cot, y_diff, y_speed, y_up, y_codes, fy, gy, hy, y_packs.at[me_y], left, right, rhs, first)
    pl.semaphore_wait(barrier, ny + nx - 2)
    y_copies = sends("yd", ny, y_packs, y_send, y_recv)
    for copy in y_copies:
        copy.start()
    for i in x_order:
        loads[i].wait()
    x_coefficients(x_diff, x_speed, x_up, coupling, x_codes, fx, gx, ix, nx_, ax, edges)
    x_chain_coefficients(edges, chain, x_coefs, me_x)
    c_copies = sends("xg", nx, x_coefs, c_send, c_recv)
    for copy in c_copies:
        copy.start()
    for copy in y_copies:
        copy.wait()
    p, q = y_interfaces(ny, y_packs, q_y, fy.shape[1])
    y_backward(p, q, fy, gy, hy, left, weights)
    x_values(weights, ix, nx_, ax, hx, edges)
    x_chain_values(edges, chain, sums, x_vals, me_x)
    v_copies = sends("xg", nx, x_vals, v_send, v_recv)
    for copy in v_copies:
        copy.start()
    for copy in c_copies:
        copy.wait()
    for copy in v_copies:
        copy.wait()
    x_backward(nx, x_coefs, x_vals, chain, sums, fx, gx, hx, out, q_x, before, own)
    stores = [pltpu.make_async_copy(out.at[c], out_hbm.at[c, 0], out_sem.at[c]) for c in range(2)]
    for copy in stores:
        copy.start()
    for copy in stores:
        copy.wait()


def per_device(ny, nx, *args):
    rows_x, length = args[0].shape[2], args[0].shape[3]
    width = 2 * rows_x // LANES
    depth = rows_x // SUB
    tall = (length * width, LANES)
    deep = (length, width, LANES)
    quad = (depth, 4, SUB, LANES)
    shapes = [
        deep, deep, deep, tall, tall, tall, (3, width, LANES), (ny, 6, width, LANES), (ny + 1, width, LANES),
        (2, rows_x, LANES), quad, quad, quad, quad, quad, (depth, 2, SUB, LANES), (24, SUB, LANES),
        (SUB, 16, LANES), (SUB, SUB, LANES), (nx, 16, LANES), (nx, SUB, LANES), (nx + 1, SUB, LANES),
        (2, SUB, LANES), (2, SUB, LANES), (2, rows_x, LANES),
    ]
    dma = pltpu.SemaphoreType.DMA
    return pl.pallas_call(
        functools.partial(kernel, ny, nx),
        out_shape=jax.ShapeDtypeStruct(args[0].shape, F32),
        in_specs=[pl.BlockSpec(memory_space=pl.ANY)] * len(args),
        out_specs=pl.BlockSpec(memory_space=pl.ANY),
        scratch_shapes=[pltpu.VMEM(a.shape, a.dtype) for a in args]
        + [pltpu.VMEM(s, F32) for s in shapes]
        + [dma((len(args),)), dma((ny - 1,)), dma((ny - 1,)), dma((nx - 1,)), dma((nx - 1,)),
           dma((nx - 1,)), dma((nx - 1,)), dma((2,))],
        compiler_params=pltpu.CompilerParams(
            collective_id=0, has_side_effects=True, vmem_limit_bytes=56 * 1024 * 1024
        ),
        name="adjoint_step",
    )(*args)


def solution(mesh):
    body = functools.partial(per_device, mesh.shape["yd"], mesh.shape["xg"])
    return jax.shard_map(
        body,
        mesh=mesh,
        in_specs=(
            P(None, None, "xg", "yd"),
            P(None, None, "xg", "yd"),
            P(None, "xg", "yd"),
            P(None, "xg", "yd"),
            P(None, None, "xg", "yd"),
            P(None, "xg", "yd"),
            P(None, "xg", "yd"),
            P(None, None, "xg", "yd"),
            P(None, "yd"),
            P(None, "xg"),
        ),
        out_specs=P(None, None, "xg", "yd"),
        check_vma=False,
    )
```

time: 41.3 us -> 19.6 us (0.47); the launches traced: 40.6 us -> 19.4 us
  local copies, waits for them, and re-layouts: 17 us -> 1.87 us
  Pallas kernels: 23.5 us -> 17.6 us
    unnamed x44 -> x1, local copies, waits for them, and re-layouts: 17 us -> 1.87 us
    pallas_call x5 -> x1, Pallas kernels: 23.5 us -> 17.6 us  [per_device(): pl.pallas_call(functools.partial(kernel, ny, nx), out_shape=jax.ShapeDtyp...]
where the time goes in v1:
time: 19.6 us; the launch traced here: 19.4 us
  Pallas kernels  17.6 us (90%)
  local copies, waits for them, and re-layouts  1.87 us (10%)
    pallas_call x1, Pallas kernels, per_device(): pl.pallas_call(functools.partial(kernel, ny, nx), out_shape=jax.ShapeDtyp...  17.6 us
    unnamed x1, local copies, waits for them, and re-layouts  1.87 us

profile of v1, /device:TPU:0, one launch (start us, length us, event | category | flops | bytes accessed | tf_op | source)
XLA Modules:
  0.0 19.4 jit_solution(2683673706019583363)
XLA Ops:
  0.0 17.6 %adjoint_step.1 = f32[2,1,512,128]{3,2,1,0:T(8,128)} custom-call(f32[2,1,512,128]{3,2,1,0:T(8,128)} %refs_0_.1, f32[2,1,512,128]{3,2,1,0:T(8,128)} %refs_1_.1, f32[1,512,128]{2,1,0:T(8,128)} %refs_2_.1, s32[1,512,128]{2,1,0:T(8,128)} %refs_3_.1, f32[2,1,512,128]{3,2,1,0:T(8,128)} %refs_4_.1, f32[1,512,128]{2,1,0:T(8,128)} %refs_5_.1, ...), custom_call_target="tpu_custom_call" | custom-call | tf_op jit(solution)/shard_map/adjoint_step/pallas_call | solution.py:449
  17.6 1.9 %copy.12 = f32[2,1,512,128]{3,2,1,0:T(8,128)} copy(f32[2,1,512,128]{3,2,1,0:T(8,128)} %adjoint_step.1) | data formatting | bytes 1048576

commit v2 on v1

--- a/solution.py
+++ b/solution.py
@@ -9,6 +9,7 @@
 
 LANES = 128
 SUB = 8
+PARTS = 4
 F32 = jnp.float32
 
 
@@ -48,7 +49,7 @@
     return carry
 
 
-def y_forward(cot, diff, speed, upwind, codes, f_out, g_out, h_out, pack, left, right, rhs, first):
+def y_forward(cot, diff, speed, upwind, codes, f_out, g_out, h_out, pack, left, right, rhs, first, joint):
     rows_x, length = cot.shape[2], cot.shape[3]
     chunks = rows_x // LANES
     width = 2 * chunks
@@ -96,15 +97,39 @@
 
     zero = jnp.zeros((width, LANES), F32)
     one = zero + 1.0
-    g, m, h, a_all, k_all, v_all = chunked(0, length - 1, 8, step, (one, zero, zero, one, zero, zero))
-    r = at(right, length - 1)
-    a0 = at(left, 0)
-    pack[0] = r * g
-    pack[1] = 1.0 + r * m
-    pack[2] = at(rhs, length - 1) + r * h
-    pack[3] = a0 * a_all
-    pack[4] = a0 * k_all
-    pack[5] = a0 * v_all
+    seg = length // PARTS
+
+    def abreast(i, carries):
+        return tuple(step(n * seg + i, c) for n, c in enumerate(carries))
+
+    start = ((one, zero, zero, one, zero, zero),) * PARTS
+    parts = []
+    for n, (g, m, h, a_all, k_all, v_all) in enumerate(chunked(0, seg - 1, 4, abreast, start)):
+        r = at(right, (n + 1) * seg - 1)
+        a0 = at(left, n * seg)
+        v = at(rhs, (n + 1) * seg - 1) + r * h
+        parts.append((r * g, 1.0 + r * m, v, a0 * a_all, a0 * k_all, a0 * v_all))
+    g, m, h = one, zero, zero
+    a_all, k_all, v_all = parts[0][3:]
+    for n in range(PARTS - 1):
+        lo, sg, v = parts[n][:3]
+        up, k_next, v_next = parts[n + 1][3:]
+        rm = (sg + k_next) + lo * m
+        rg = lo * g
+        inv = 1.0 / ((rm + up) + rg)
+        m = rm * inv
+        g = rg * inv
+        h = ((v + v_next) + lo * h) * inv
+        f = up * inv
+        joint[n, 0] = f
+        joint[n, 1] = g
+        joint[n, 2] = h
+        k_all = k_all + a_all * m
+        v_all = v_all + a_all * h
+        a_all = a_all * f
+    lo, sg, v = parts[-1][:3]
+    for e, value in enumerate((lo * g, sg + lo * m, v + lo * h, a_all, k_all, v_all)):
+        pack[e] = value
 
 
 def y_interfaces(ny, packs, q_all, width):
@@ -133,21 +158,30 @@
     return q_all[me], q_all[me + 1]
 
 
-def y_backward(p, q, fy, gy, hy, lines, weights):
+def y_backward(p, q, fy, gy, hy, joint, lines, weights):
     length, width = fy.shape[0], fy.shape[1]
 
     def put(i, value):
         lines[pl.ds(pl.multiple_of(i * width, width), width), :] = value
 
-    put(length - 1, q)
-
-    def back(n, w):
-        i = length - 2 - n
-        w = fy[i] * w + (gy[i] * p + hy[i])
-        put(i, w)
-        return w
-
-    chunked(0, length - 1, 8, back, q)
+    seg = length // PARTS
+    ends = [q]
+    for n in reversed(range(PARTS - 1)):
+        ends.insert(0, joint[n, 0] * ends[0] + (joint[n, 1] * p + joint[n, 2]))
+    starts = [p] + ends[:-1]
+    for n in range(PARTS):
+        put((n + 1) * seg - 1, ends[n])
+
+    def back(k, ws):
+        done = []
+        for n, w in enumerate(ws):
+            i = (n + 1) * seg - 2 - k
+            w = fy[i] * w + (gy[i] * starts[n] + hy[i])
+            put(i, w)
+            done.append(w)
+        return tuple(done)
+
+    chunked(0, seg - 1, 4, back, tuple(ends))
     chunks = width // 2
     for c in range(2):
         for j in range(chunks):
@@ -155,7 +189,7 @@
             weights[c, pl.ds(j * LANES, LANES), :] = block.T
 
 
-def x_coefficients(diff, speed, upwind, coupling, codes, fx, gx, ix, nx_, ax, edges):
+def x_coefficients(diff, speed, upwind, coupling, codes, fx, gx, ix, nx_, ax, halves, edges):
     depth = diff.shape[2] // SUB
     at_start = lax.axis_index("xg") == 0
 
@@ -209,27 +243,53 @@
     vented = (kind >= 1).astype(F32)
     opened = (kind == 1).astype(F32)
     r_first = tuple(jnp.where(top, vented * sn + opened * d, sn + d) for d in (d0, d1))
-    carry = step(0, (unit, none, unit, none), r_first)
-
-    def inner(k, c):
+    half = depth // 2
+
+    def plain(k):
         sn, d0, d1 = rights(k)
-        return step(k, c, (sn + d0, sn + d1))
-
-    g, m, a_all, k_all = chunked(1, depth - 1, 2, inner, carry)
-    sn, d0, d1 = rights(depth - 1)
-    r = (sn + d0, sn + d1)
-    sg = sigma(depth - 1)
-    rr = (r[0], r[0], r[1], r[1])
-    a0 = lefts(0)
-    aa = (a0[0], a0[0], a0[1], a0[1])
+        return (sn + d0, sn + d1)
+
+    def abreast(k, cs):
+        return (step(k, cs[0], plain(k)), step(half + k, cs[1], plain(half + k)))
+
+    fresh = (unit, none, unit, none)
+    pair = (step(0, fresh, r_first), step(half, fresh, plain(half)))
+    pair = chunked(1, half - 1, 2, abreast, pair)
+    ends = []
+    for n, (g, m, a_all, k_all) in enumerate(pair):
+        end = (n + 1) * half - 1
+        r = plain(end)
+        rr = (r[0], r[0], r[1], r[1])
+        a0 = lefts(n * half)
+        aa = (a0[0], a0[0], a0[1], a0[1])
+        sg = sigma(end)
+        for c in range(2):
+            halves[20 + 4 * n + c] = a0[c]
+            halves[22 + 4 * n + c] = r[c]
+        ends.append((
+            tuple(x * y for x, y in zip(rr, g)),
+            tuple(z + x * y for x, y, z in zip(rr, m, sg)),
+            tuple(x * y for x, y in zip(aa, a_all)),
+            tuple(x * y for x, y in zip(aa, k_all)),
+        ))
+    (lo, sg, a_all, k_all), (lo_end, sg_end, up, k_next) = ends
+    sg = add(sg, k_next)
+    inv = mat_inv(add(add(sg, lo), up))
+    m, g, f = mat_mul(inv, sg), mat_mul(inv, lo), mat_mul(inv, up)
+    lo_sub = mat_mul(lo_end, g)
+    sg_sub = add(sg_end, mat_mul(lo_end, m))
+    k_sub = add(k_all, mat_mul(a_all, m))
+    a_sub = mat_mul(a_all, f)
     for e in range(4):
-        edges[e] = rr[e] * g[e]
-        edges[4 + e] = sg[e] + rr[e] * m[e]
-        edges[8 + e] = aa[e] * a_all[e]
-        edges[12 + e] = aa[e] * k_all[e]
-    for c in range(2):
-        edges[20 + c] = a0[c]
-        edges[22 + c] = r[c]
+        halves[e] = f[e]
+        halves[4 + e] = g[e]
+        halves[8 + e] = inv[e]
+        halves[12 + e] = lo_end[e]
+        halves[16 + e] = a_all[e]
+        edges[e] = lo_sub[e]
+        edges[4 + e] = sg_sub[e]
+        edges[8 + e] = a_sub[e]
+        edges[12 + e] = k_sub[e]
 
 
 def edge_rows(edges, first, n, s):
@@ -261,25 +321,46 @@
         pack[me, pl.ds(e, 1), :] = row
 
 
-def x_values(weights, ix, nx_, ax, hx, edges):
+def x_values(weights, ix, nx_, ax, hx, halves, edges):
     depth = weights.shape[1] // SUB
+    half = depth // 2
+
+    def at(k):
+        return tuple(weights[c, pl.ds(k, SUB, stride=depth), :] for c in range(2))
+
+    def quad(ref, k):
+        return tuple(ref[k, e] for e in range(4))
+
+    def held(first, n):
+        return tuple(halves[first + e] for e in range(n))
 
     def step(k, carry):
         h, v_all = carry
-        w = tuple(weights[c, pl.ds(k, SUB, stride=depth), :] for c in range(2))
-        base = mat_vec(tuple(ix[k, e] for e in range(4)), w)
-        n = tuple(nx_[k, e] for e in range(4))
-        a_all = tuple(ax[k, e] for e in range(4))
+        base = mat_vec(quad(ix, k), at(k))
+        n = quad(nx_, k)
         h = ((base[0] + n[0] * h[0]) + n[1] * h[1], (base[1] + n[2] * h[0]) + n[3] * h[1])
         for c in range(2):
             hx[k, c] = h[c]
-        return h, add(v_all, mat_vec(a_all, h))
+        return h, add(v_all, mat_vec(quad(ax, k), h))
+
+    def abreast(k, cs):
+        return (step(k, cs[0]), step(half + k, cs[1]))
 
     zero = jnp.zeros((SUB, LANES), F32)
-    h, v_all = chunked(0, depth - 1, 7, step, ((zero, zero), (zero, zero)))
+    fresh = ((zero, zero), (zero, zero))
+    ends = []
+    for n, (h, v_all) in enumerate(chunked(0, half - 1, 4, abreast, (fresh, fresh))):
+        a0, r = held(20 + 4 * n, 2), held(22 + 4 * n, 2)
+        w = at((n + 1) * half - 1)
+        ends.append((tuple(w[c] + r[c] * h[c] for c in range(2)), tuple(a0[c] * v_all[c] for c in range(2))))
+    (v, v_all), (v_end, v_next) = ends
+    h = mat_vec(held(8, 4), add(v, v_next))
+    v_end = add(v_end, mat_vec(held(12, 4), h))
+    v_all = add(v_all, mat_vec(held(16, 4), h))
     for c in range(2):
-        edges[16 + c] = weights[c, pl.ds(depth - 1, SUB, stride=depth), :] + edges[22 + c] * h[c]
-        edges[18 + c] = edges[20 + c] * v_all[c]
+        halves[28 + c] = h[c]
+        edges[16 + c] = v_end[c]
+        edges[18 + c] = v_all[c]
 
 
 def x_chain_values(edges, chain, sums, pack, me):
@@ -301,7 +382,7 @@
         pack[me, pl.ds(e, 1), :] = sent[e] if e < len(sent) else zrow
 
 
-def x_backward(nx, coefs, values, chain, sums, fx, gx, hx, out, q_all, before, own):
+def x_backward(nx, coefs, values, chain, sums, halves, fx, gx, hx, out, q_all, before, own):
     def row(ref, j, first, n):
         return tuple(ref[j, pl.ds(first + e, 1), :] for e in range(n))
 
@@ -343,26 +424,35 @@
         for c in range(2):
             own[c, pl.ds(s, 1), :] = q[c]
             before[c, pl.ds(s + 1, 1), :] = q[c]
-    depth = out.shape[1] // SUB
+    depth = out.shape[2] // SUB
+    half = depth // 2
     prev = (before[0], before[1])
     x = (own[0], own[1])
 
+    def held(first, n):
+        return tuple(halves[first + e] for e in range(n))
+
+    mid = add(mat_vec(held(0, 4), x), add(mat_vec(held(4, 4), prev), held(28, 2)))
+
     def put(k, x):
         for c in range(2):
-            out[c, pl.ds(k, SUB, stride=depth), :] = x[c]
+            out[c, 0, pl.ds(k, SUB, stride=depth), :] = x[c]
 
     put(depth - 1, x)
-
-    def back(n, x):
-        k = depth - 2 - n
+    put(half - 1, mid)
+
+    def solve(k, x, start):
         f = tuple(fx[k, e] for e in range(4))
         g = tuple(gx[k, e] for e in range(4))
-        base = add(mat_vec(g, prev), (hx[k, 0], hx[k, 1]))
-        x = add(mat_vec(f, x), base)
+        base = add(mat_vec(g, start), (hx[k, 0], hx[k, 1]))
+        x = ((base[0] + f[0] * x[0]) + f[1] * x[1], (base[1] + f[2] * x[0]) + f[3] * x[1])
         put(k, x)
         return x
 
-    chunked(0, depth - 1, 8, back, x)
+    def back(n, xs):
+        return (solve(half - 2 - n, xs[0], prev), solve(depth - 2 - n, xs[1], mid))
+
+    chunked(0, half - 1, 4, back, (mid, x))
 
 
 def sends(axis, count, ref, send_sem, recv_sem):
@@ -381,11 +471,11 @@
 
 
 def kernel(ny, nx, *refs):
-    sources, out_hbm = refs[:10], refs[10]
+    sources, out = refs[:10], refs[10]
     held = refs[11:21]
     (fy, gy, hy, left, right, rhs, first, y_packs, q_y, weights, fx, gx, ix, nx_, ax, hx, edges,
-     chain, sums, x_coefs, x_vals, q_x, before, own, out,
-     in_sem, y_send, y_recv, c_send, c_recv, v_send, v_recv, out_sem) = refs[21:]
+     chain, sums, x_coefs, x_vals, q_x, before, own, joint, halves,
+     in_sem, y_send, y_recv, c_send, c_recv, v_send, v_recv) = refs[21:]
     cot, x_diff, x_speed, x_up, y_diff, y_speed, y_up, coupling, x_codes, y_codes = held
     loads = [pltpu.make_async_copy(s, d, in_sem.at[i]) for i, (s, d) in enumerate(zip(sources, held))]
     y_order, x_order = (5, 6, 4, 0, 9), (2, 3, 1, 7, 8)
@@ -399,14 +489,14 @@
     for i in y_order:
         loads[i].wait()
     me_y, me_x = lax.axis_index("yd"), lax.axis_index("xg")
-    y_forward(cot, y_diff, y_speed, y_up, y_codes, fy, gy, hy, y_packs.at[me_y], left, right, rhs, first)
+    y_forward(cot, y_diff, y_speed, y_up, y_codes, fy, gy, hy, y_packs.at[me_y], left, right, rhs, first, joint)
     pl.semaphore_wait(barrier, ny + nx - 2)
     y_copies = sends("yd", ny, y_packs, y_send, y_recv)
     for copy in y_copies:
         copy.start()
     for i in x_order:
         loads[i].wait()
-    x_coefficients(x_diff, x_speed, x_up, coupling, x_codes, fx, gx, ix, nx_, ax, edges)
+    x_coefficients(x_diff, x_speed, x_up, coupling, x_codes, fx, gx, ix, nx_, ax, halves, edges)
     x_chain_coefficients(edges, chain, x_coefs, me_x)
     c_copies = sends("xg", nx, x_coefs, c_send, c_recv)
     for copy in c_copies:
@@ -414,8 +504,8 @@
     for copy in y_copies:
         copy.wait()
     p, q = y_interfaces(ny, y_packs, q_y, fy.shape[1])
-    y_backward(p, q, fy, gy, hy, left, weights)
-    x_values(weights, ix, nx_, ax, hx, edges)
+    y_backward(p, q, fy, gy, hy, joint, left, weights)
+    x_values(weights, ix, nx_, ax, hx, halves, edges)
     x_chain_values(edges, chain, sums, x_vals, me_x)
     v_copies = sends("xg", nx, x_vals, v_send, v_recv)
     for copy in v_copies:
@@ -424,12 +514,7 @@
         copy.wait()
     for copy in v_copies:
         copy.wait()
-    x_backward(nx, x_coefs, x_vals, chain, sums, fx, gx, hx, out, q_x, before, own)
-    stores = [pltpu.make_async_copy(out.at[c], out_hbm.at[c, 0], out_sem.at[c]) for c in range(2)]
-    for copy in stores:
-        copy.start()
-    for copy in stores:
-        copy.wait()
+    x_backward(nx, x_coefs, x_vals, chain, sums, halves, fx, gx, hx, out, q_x, before, own)
 
 
 def per_device(ny, nx, *args):
@@ -443,18 +528,18 @@
         deep, deep, deep, tall, tall, tall, (3, width, LANES), (ny, 6, width, LANES), (ny + 1, width, LANES),
         (2, rows_x, LANES), quad, quad, quad, quad, quad, (depth, 2, SUB, LANES), (24, SUB, LANES),
         (SUB, 16, LANES), (SUB, SUB, LANES), (nx, 16, LANES), (nx, SUB, LANES), (nx + 1, SUB, LANES),
-        (2, SUB, LANES), (2, SUB, LANES), (2, rows_x, LANES),
+        (2, SUB, LANES), (2, SUB, LANES), (PARTS - 1, 3, width, LANES), (30, SUB, LANES),
     ]
     dma = pltpu.SemaphoreType.DMA
     return pl.pallas_call(
         functools.partial(kernel, ny, nx),
         out_shape=jax.ShapeDtypeStruct(args[0].shape, F32),
         in_specs=[pl.BlockSpec(memory_space=pl.ANY)] * len(args),
-        out_specs=pl.BlockSpec(memory_space=pl.ANY),
+        out_specs=pl.BlockSpec(memory_space=pltpu.VMEM),
         scratch_shapes=[pltpu.VMEM(a.shape, a.dtype) for a in args]
         + [pltpu.VMEM(s, F32) for s in shapes]
         + [dma((len(args),)), dma((ny - 1,)), dma((ny - 1,)), dma((nx - 1,)), dma((nx - 1,)),
-           dma((nx - 1,)), dma((nx - 1,)), dma((2,))],
+           dma((nx - 1,)), dma((nx - 1,))],
         compiler_params=pltpu.CompilerParams(
             collective_id=0, has_side_effects=True, vmem_limit_bytes=56 * 1024 * 1024
         ),

time: 19.6 us -> 18.6 us (0.949)
  Pallas kernels: 17.6 us -> 16.6 us
    pallas_call x1, Pallas kernels: 17.6 us -> 16.6 us  [per_device(): pl.pallas_call(functools.partial(kernel, ny, nx), out_shape=jax.ShapeDtyp...]
where the time goes in v2:
time: 18.6 us; the launch traced here: 18.5 us
  Pallas kernels  16.6 us (89%)
  local copies, waits for them, and re-layouts  1.87 us (10%)
    pallas_call x1, Pallas kernels, per_device(): pl.pallas_call(functools.partial(kernel, ny, nx), out_shape=jax.ShapeDtyp...  16.6 us
    unnamed x1, local copies, waits for them, and re-layouts  1.87 us

profile of v2, /device:TPU:0, one launch (start us, length us, event | category | flops | bytes accessed | tf_op | source)
XLA Modules:
  0.0 18.5 jit_solution(13997067805456335276)
XLA Ops:
  0.0 16.6 %adjoint_step.1 = f32[2,1,512,128]{3,2,1,0:T(8,128)} custom-call(f32[2,1,512,128]{3,2,1,0:T(8,128)} %refs_0_.1, f32[2,1,512,128]{3,2,1,0:T(8,128)} %refs_1_.1, f32[1,512,128]{2,1,0:T(8,128)} %refs_2_.1, s32[1,512,128]{2,1,0:T(8,128)} %refs_3_.1, f32[2,1,512,128]{3,2,1,0:T(8,128)} %refs_4_.1, f32[1,512,128]{2,1,0:T(8,128)} %refs_5_.1, ...), custom_call_target="tpu_custom_call" | custom-call | tf_op jit(solution)/shard_map/adjoint_step/pallas_call | solution.py:534
  16.6 1.9 %copy.12 = f32[2,1,512,128]{3,2,1,0:T(8,128)} copy(f32[2,1,512,128]{3,2,1,0:T(8,128)} %adjoint_step.1) | data formatting | bytes 1048576

commit v3 on v2

--- a/solution.py
+++ b/solution.py
@@ -10,6 +10,7 @@
 LANES = 128
 SUB = 8
 PARTS = 4
+GROUPS = 2
 F32 = jnp.float32
 
 
@@ -49,12 +50,15 @@
     return carry
 
 
-def y_forward(cot, diff, speed, upwind, codes, f_out, g_out, h_out, pack, left, right, rhs, first, joint):
+def y_forward(cot, diff, speed, upwind, codes, f_out, g_out, h_out, pack, left, right, rhs, first, joint, arrived):
     rows_x, length = cot.shape[2], cot.shape[3]
     chunks = rows_x // LANES
     width = 2 * chunks
     boundary = lax.axis_index("yd") == 0
     for j in range(chunks):
+        if j % (chunks // GROUPS) == 0:
+            for copy in arrived[j // (chunks // GROUPS)]:
+                copy.wait()
         span = pl.ds(j * LANES, LANES)
         sp = speed[0, span, :]
         sm = sp * upwind[0, span, :].astype(F32)
@@ -66,7 +70,7 @@
             where = pl.ds(slot, length, stride=width)
             left[where, :] = smt + df
             right[where, :] = snt + df
-            rhs[where, :] = cot[c, 0, span, :].T
+            rhs[where, :] = 2.0 * cot[c, 0, span, :].T
             first[0, pl.ds(slot, 1), :] = snt[0:1, :]
             first[1, pl.ds(slot, 1), :] = df[0:1, :]
             first[2, pl.ds(slot, 1), :] = codes[0:1, span].astype(F32)
@@ -477,25 +481,34 @@
      chain, sums, x_coefs, x_vals, q_x, before, own, joint, halves,
      in_sem, y_send, y_recv, c_send, c_recv, v_send, v_recv) = refs[21:]
     cot, x_diff, x_speed, x_up, y_diff, y_speed, y_up, coupling, x_codes, y_codes = held
-    loads = [pltpu.make_async_copy(s, d, in_sem.at[i]) for i, (s, d) in enumerate(zip(sources, held))]
-    y_order, x_order = (5, 6, 4, 0, 9), (2, 3, 1, 7, 8)
-    for i in y_order + x_order:
-        loads[i].start()
+    count = sources[0].shape[2] // GROUPS
+    arrived = []
+    for n in range(GROUPS):
+        part = pl.ds(n * count, count)
+        group = []
+        for e, i in enumerate((5, 6, 4, 0)):
+            where = (slice(None),) * (1 if i in (5, 6) else 2) + (part,)
+            sem = in_sem.at[n * 4 + e]
+            group.append(pltpu.make_async_copy(sources[i].at[where], held[i].at[where], sem))
+        arrived.append(group)
+    order = (9, 2, 3, 1, 7, 8)
+    rest = [pltpu.make_async_copy(sources[i], held[i], in_sem.at[4 * GROUPS + e]) for e, i in enumerate(order)]
+    arrived[0].append(rest[0])
+    for copy in arrived[0] + sum(arrived[1:], []) + rest[1:]:
+        copy.start()
     barrier = pltpu.get_barrier_semaphore()
     for axis, count in (("yd", ny), ("xg", nx)):
         for k in range(1, count):
             peer = lax.rem(lax.axis_index(axis) + k, count)
             pl.semaphore_signal(barrier, inc=1, device_id={axis: peer}, device_id_type=pl.DeviceIdType.MESH)
-    for i in y_order:
-        loads[i].wait()
     me_y, me_x = lax.axis_index("yd"), lax.axis_index("xg")
-    y_forward(cot, y_diff, y_speed, y_up, y_codes, fy, gy, hy, y_packs.at[me_y], left, right, rhs, first, joint)
+    y_forward(cot, y_diff, y_speed, y_up, y_codes, fy, gy, hy, y_packs.at[me_y], left, right, rhs, first, joint, arrived)
     pl.semaphore_wait(barrier, ny + nx - 2)
     y_copies = sends("yd", ny, y_packs, y_send, y_recv)
     for copy in y_copies:
         copy.start()
-    for i in x_order:
-        loads[i].wait()
+    for copy in rest[1:]:
+        copy.wait()
     x_coefficients(x_diff, x_speed, x_up, coupling, x_codes, fx, gx, ix, nx_, ax, halves, edges)
     x_chain_coefficients(edges, chain, x_coefs, me_x)
     c_copies = sends("xg", nx, x_coefs, c_send, c_recv)
@@ -531,20 +544,21 @@
         (2, SUB, LANES), (2, SUB, LANES), (PARTS - 1, 3, width, LANES), (30, SUB, LANES),
     ]
     dma = pltpu.SemaphoreType.DMA
-    return pl.pallas_call(
+    doubled = pl.pallas_call(
         functools.partial(kernel, ny, nx),
         out_shape=jax.ShapeDtypeStruct(args[0].shape, F32),
         in_specs=[pl.BlockSpec(memory_space=pl.ANY)] * len(args),
         out_specs=pl.BlockSpec(memory_space=pltpu.VMEM),
         scratch_shapes=[pltpu.VMEM(a.shape, a.dtype) for a in args]
         + [pltpu.VMEM(s, F32) for s in shapes]
-        + [dma((len(args),)), dma((ny - 1,)), dma((ny - 1,)), dma((nx - 1,)), dma((nx - 1,)),
+        + [dma((4 * GROUPS + 6,)), dma((ny - 1,)), dma((ny - 1,)), dma((nx - 1,)), dma((nx - 1,)),
            dma((nx - 1,)), dma((nx - 1,))],
         compiler_params=pltpu.CompilerParams(
             collective_id=0, has_side_effects=True, vmem_limit_bytes=56 * 1024 * 1024
         ),
         name="adjoint_step",
     )(*args)
+    return 0.5 * doubled
 
 
 def solution(mesh):

time: 18.6 us -> 18.5 us (level)
  other arithmetic: 0 us -> 1.87 us
  local copies, waits for them, and re-layouts: 1.87 us -> 0 us
    mul x0 -> x1, other arithmetic: none -> 1.87 us  [per_device(): return 0.5 * doubled]
    unnamed x1 -> x0, local copies, waits for them, and re-layouts: 1.87 us -> none
where the time goes in v3:
time: 18.5 us; the launch traced here: 18.4 us
  Pallas kernels  16.5 us (89%)
  other arithmetic  1.87 us (10%)
    pallas_call x1, Pallas kernels, per_device(): pl.pallas_call(functools.partial(kernel, ny, nx), out_shape=jax.ShapeDtyp...  16.5 us
    mul x1, other arithmetic, per_device(): return 0.5 * doubled  1.87 us

profile of v3, /device:TPU:0, one launch (start us, length us, event | category | flops | bytes accessed | tf_op | source)
XLA Modules:
  0.0 18.4 jit_solution(2592708175290233470)
XLA Ops:
  0.0 16.5 %adjoint_step.1 = f32[2,1,512,128]{3,2,1,0:T(8,128)} custom-call(f32[2,1,512,128]{3,2,1,0:T(8,128)} %refs_0_.1, f32[2,1,512,128]{3,2,1,0:T(8,128)} %refs_1_.1, f32[1,512,128]{2,1,0:T(8,128)} %refs_2_.1, s32[1,512,128]{2,1,0:T(8,128)} %refs_3_.1, f32[2,1,512,128]{3,2,1,0:T(8,128)} %refs_4_.1, f32[1,512,128]{2,1,0:T(8,128)} %refs_5_.1, ...), custom_call_target="tpu_custom_call" | custom-call | tf_op jit(solution)/shard_map/adjoint_step/pallas_call | solution.py:547
  16.5 1.9 %broadcast_multiply_fusion = f32[2,1,512,128]{3,2,1,0:T(8,128)} fusion(f32[2,1,512,128]{3,2,1,0:T(8,128)} %adjoint_step.1), kind=kLoop, calls=%fused_computation | loop fusion | flops 131072 | bytes 1048576 | tf_op jit(solution)/shard_map/mul | solution.py:561

commit v4 on v2

--- a/solution.py
+++ b/solution.py
@@ -517,6 +517,33 @@
     x_backward(nx, x_coefs, x_vals, chain, sums, halves, fx, gx, hx, out, q_x, before, own)
 
 
+PIECES = 8
+
+
+def hand_kernel(src, out, sem):
+    rows = src.shape[2] // (PIECES // 2)
+    copies = []
+    for n in range(PIECES):
+        where = (n % 2, 0, pl.ds(n // 2 * rows, rows))
+        copies.append(pltpu.make_async_copy(src.at[where], out.at[where], sem.at[n]))
+    for copy in copies:
+        copy.start()
+    for copy in copies:
+        copy.wait()
+
+
+def handed_on(block):
+    return pl.pallas_call(
+        hand_kernel,
+        out_shape=jax.ShapeDtypeStruct(block.shape, block.dtype),
+        in_specs=[pl.BlockSpec(memory_space=pl.ANY)],
+        out_specs=pl.BlockSpec(memory_space=pl.ANY),
+        scratch_shapes=[pltpu.SemaphoreType.DMA((PIECES,))],
+        compiler_params=pltpu.CompilerParams(vmem_limit_bytes=61 * 1024 * 1024),
+        name="hand_on",
+    )(block)
+
+
 def per_device(ny, nx, *args):
     rows_x, length = args[0].shape[2], args[0].shape[3]
     width = 2 * rows_x // LANES
@@ -531,7 +558,7 @@
         (2, SUB, LANES), (2, SUB, LANES), (PARTS - 1, 3, width, LANES), (30, SUB, LANES),
     ]
     dma = pltpu.SemaphoreType.DMA
-    return pl.pallas_call(
+    solved = pl.pallas_call(
         functools.partial(kernel, ny, nx),
         out_shape=jax.ShapeDtypeStruct(args[0].shape, F32),
         in_specs=[pl.BlockSpec(memory_space=pl.ANY)] * len(args),
@@ -545,6 +572,7 @@
         ),
         name="adjoint_step",
     )(*args)
+    return handed_on(solved)
 
 
 def solution(mesh):

time: 18.6 us -> 33.8 us (1.82)
  Pallas kernels: 16.6 us -> 33.6 us
  local copies, waits for them, and re-layouts: 1.87 us -> 0 us
    pallas_call x0 -> x1, Pallas kernels: none -> 17.1 us  [handed_on(): pl.pallas_call(hand_kernel, out_shape=jax.ShapeDtypeStruct(block.shape, b...]
    unnamed x1 -> x0, local copies, waits for them, and re-layouts: 1.87 us -> none
where the time goes in v4:
time: 33.8 us; the launch traced here: 33.7 us
  Pallas kernels  33.6 us (99%)
    pallas_call x1, Pallas kernels, handed_on(): pl.pallas_call(hand_kernel, out_shape=jax.ShapeDtypeStruct(block.shape, b...  17.1 us
    pallas_call x1, Pallas kernels, per_device(): pl.pallas_call(functools.partial(kernel, ny, nx), out_shape=jax.ShapeDtyp...  16.6 us

profile of v4, /device:TPU:0, one launch (start us, length us, event | category | flops | bytes accessed | tf_op | source)
XLA Modules:
  0.0 33.7 jit_solution(7460436629170954207)
XLA Ops:
  0.0 16.6 %adjoint_step.1.src = f32[2,1,512,128]{3,2,1,0:T(8,128)} custom-call(f32[2,1,512,128]{3,2,1,0:T(8,128)} %refs_0_.1, f32[2,1,512,128]{3,2,1,0:T(8,128)} %refs_1_.1, f32[1,512,128]{2,1,0:T(8,128)} %refs_2_.1, s32[1,512,128]{2,1,0:T(8,128)} %refs_3_.1, f32[2,1,512,128]{3,2,1,0:T(8,128)} %refs_4_.1, f32[1,512,128]{2,1,0:T(8,128)} %refs_5_.1, ...), custom_call_target="tpu_custom_call" | custom-call | tf_op jit(solution)/shard_map/adjoint_step/pallas_call | solution.py:561
  16.6 17.1 %hand_on.1 = f32[2,1,512,128]{3,2,1,0:T(8,128)} custom-call(f32[2,1,512,128]{3,2,1,0:T(8,128)} %adjoint_step.1.src), custom_call_target="tpu_custom_call" | custom-call | tf_op jit(solution)/shard_map/hand_on/pallas_call | solution.py:536

commit v5 on v4

--- a/solution.py
+++ b/solution.py
@@ -517,18 +517,22 @@
     x_backward(nx, x_coefs, x_vals, chain, sums, halves, fx, gx, hx, out, q_x, before, own)
 
 
-PIECES = 8
-
-
-def hand_kernel(src, out, sem):
+PIECES = 4
+
+
+def hand_kernel(src, out, held, in_sem, out_sem):
     rows = src.shape[2] // (PIECES // 2)
-    copies = []
+    loads, stores = [], []
     for n in range(PIECES):
         where = (n % 2, 0, pl.ds(n // 2 * rows, rows))
-        copies.append(pltpu.make_async_copy(src.at[where], out.at[where], sem.at[n]))
-    for copy in copies:
+        loads.append(pltpu.make_async_copy(src.at[where], held.at[n], in_sem.at[n]))
+        stores.append(pltpu.make_async_copy(held.at[n], out.at[where], out_sem.at[n]))
+    for copy in loads:
         copy.start()
-    for copy in copies:
+    for load, store in zip(loads, stores):
+        load.wait()
+        store.start()
+    for copy in stores:
         copy.wait()
 
 
@@ -538,7 +542,11 @@
         out_shape=jax.ShapeDtypeStruct(block.shape, block.dtype),
         in_specs=[pl.BlockSpec(memory_space=pl.ANY)],
         out_specs=pl.BlockSpec(memory_space=pl.ANY),
-        scratch_shapes=[pltpu.SemaphoreType.DMA((PIECES,))],
+        scratch_shapes=[
+            pltpu.VMEM((PIECES, block.shape[2] // (PIECES // 2), block.shape[3]), block.dtype),
+            pltpu.SemaphoreType.DMA((PIECES,)),
+            pltpu.SemaphoreType.DMA((PIECES,)),
+        ],
         compiler_params=pltpu.CompilerParams(vmem_limit_bytes=61 * 1024 * 1024),
         name="hand_on",
     )(block)

time: 33.8 us -> 18.6 us (0.55)
  Pallas kernels: 33.6 us -> 18.4 us
    pallas_call x1, Pallas kernels: 17.1 us -> 1.82 us  [handed_on(): pl.pallas_call(hand_kernel, out_shape=jax.ShapeDtypeStruct(block.shape, b...]
where the time goes in v5:
time: 18.6 us; the launch traced here: 18.4 us
  Pallas kernels  18.4 us (99%)
    pallas_call x1, Pallas kernels, per_device(): pl.pallas_call(functools.partial(kernel, ny, nx), out_shape=jax.ShapeDtyp...  16.6 us
    pallas_call x1, Pallas kernels, handed_on(): pl.pallas_call(hand_kernel, out_shape=jax.ShapeDtypeStruct(block.shape, b...  1.82 us

profile of v5, /device:TPU:0, one launch (start us, length us, event | category | flops | bytes accessed | tf_op | source)
XLA Modules:
  0.0 18.4 jit_solution(8308524559718082572)
XLA Ops:
  0.0 16.6 %adjoint_step.1.src = f32[2,1,512,128]{3,2,1,0:T(8,128)} custom-call(f32[2,1,512,128]{3,2,1,0:T(8,128)} %refs_0_.1, f32[2,1,512,128]{3,2,1,0:T(8,128)} %refs_1_.1, f32[1,512,128]{2,1,0:T(8,128)} %refs_2_.1, s32[1,512,128]{2,1,0:T(8,128)} %refs_3_.1, f32[2,1,512,128]{3,2,1,0:T(8,128)} %refs_4_.1, f32[1,512,128]{2,1,0:T(8,128)} %refs_5_.1, ...), custom_call_target="tpu_custom_call" | custom-call | tf_op jit(solution)/shard_map/adjoint_step/pallas_call | solution.py:569
  16.6 1.8 %hand_on.1 = f32[2,1,512,128]{3,2,1,0:T(8,128)} custom-call(f32[2,1,512,128]{3,2,1,0:T(8,128)} %adjoint_step.1.src), custom_call_target="tpu_custom_call" | custom-call | tf_op jit(solution)/shard_map/hand_on/pallas_call | solution.py:540

commit v6 on v2

--- a/solution.py
+++ b/solution.py
@@ -382,26 +382,32 @@
         pack[me, pl.ds(e, 1), :] = sent[e] if e < len(sent) else zrow
 
 
-def x_backward(nx, coefs, values, chain, sums, halves, fx, gx, hx, out, q_all, before, own):
+def x_backward(nx, coefs, values, v_copies, chain, sums, halves, fx, gx, hx, out, q_all, before, own):
     def row(ref, j, first, n):
         return tuple(ref[j, pl.ds(first + e, 1), :] for e in range(n))
 
     zrow = jnp.zeros((1, LANES), F32)
     orow = zrow + 1.0
     slack, h = (orow, zrow, zrow, orow), (zrow, zrow)
-    factors = []
+    solvers, factors = [], []
     for j in range(nx):
-        lo, sg, v = row(coefs, j, 0, 4), row(coefs, j, 4, 4), row(values, j, 0, 2)
+        lo, sg = row(coefs, j, 0, 4), row(coefs, j, 4, 4)
         up = (zrow,) * 4
         if j + 1 < nx:
             up = row(coefs, j + 1, 8, 4)
             sg = add(sg, row(coefs, j + 1, 12, 4))
-            v = add(v, row(values, j + 1, 2, 2))
         t = add(sg, mat_mul(lo, slack))
         inv = mat_inv(add(t, up))
         slack = mat_mul(inv, t)
+        solvers.append((lo, inv, mat_mul(inv, up)))
+    for copy in v_copies:
+        copy.wait()
+    for j, (lo, inv, f) in enumerate(solvers):
+        v = row(values, j, 0, 2)
+        if j + 1 < nx:
+            v = add(v, row(values, j + 1, 2, 2))
         h = mat_vec(inv, add(v, mat_vec(lo, h)))
-        factors.append((mat_mul(inv, up), h))
+        factors.append((f, h))
     q = (zrow, zrow)
     for c in range(2):
         q_all[0, pl.ds(c, 1), :] = zrow
@@ -512,9 +518,7 @@
         copy.start()
     for copy in c_copies:
         copy.wait()
-    for copy in v_copies:
-        copy.wait()
-    x_backward(nx, x_coefs, x_vals, chain, sums, halves, fx, gx, hx, out, q_x, before, own)
+    x_backward(nx, x_coefs, x_vals, v_copies, chain, sums, halves, fx, gx, hx, out, q_x, before, own)
 
 
 def per_device(ny, nx, *args):

time: 18.6 us -> 18.6 us (level)
  no operation moved by 1% of the time
where the time goes in v6:
time: 18.6 us; the launch traced here: 18.4 us
  Pallas kernels  16.5 us (89%)
  local copies, waits for them, and re-layouts  1.87 us (10%)
    pallas_call x1, Pallas kernels, per_device(): pl.pallas_call(functools.partial(kernel, ny, nx), out_shape=jax.ShapeDtyp...  16.5 us
    unnamed x1, local copies, waits for them, and re-layouts  1.87 us

profile of v6, /device:TPU:0, one launch (start us, length us, event | category | flops | bytes accessed | tf_op | source)
XLA Modules:
  0.0 18.4 jit_solution(10243180498122125778)
XLA Ops:
  0.0 16.5 %adjoint_step.1 = f32[2,1,512,128]{3,2,1,0:T(8,128)} custom-call(f32[2,1,512,128]{3,2,1,0:T(8,128)} %refs_0_.1, f32[2,1,512,128]{3,2,1,0:T(8,128)} %refs_1_.1, f32[1,512,128]{2,1,0:T(8,128)} %refs_2_.1, s32[1,512,128]{2,1,0:T(8,128)} %refs_3_.1, f32[2,1,512,128]{3,2,1,0:T(8,128)} %refs_4_.1, f32[1,512,128]{2,1,0:T(8,128)} %refs_5_.1, ...), custom_call_target="tpu_custom_call" | custom-call | tf_op jit(solution)/shard_map/adjoint_step/pallas_call | solution.py:538
  16.5 1.9 %copy.12 = f32[2,1,512,128]{3,2,1,0:T(8,128)} copy(f32[2,1,512,128]{3,2,1,0:T(8,128)} %adjoint_step.1) | data formatting | bytes 1048576
